TPU v7x, 32 devices: a whole 2x2x4 slice. The times are simulated.
32 devices in a mesh: ctx: 4 (over y, x), wa: 8 (over z, core).
Axes of the slice: x: 2, y: 2, z: 4, core: 2. Of those that a mesh axis runs over, the one named last changes fastest.
Arguments:
- block_input: float32 [8, 512, 2048], P('wa', 'ctx'), may hold values from -6 to 6
- query_weight: bfloat16 [2048, 4096], P('wa'), may hold values from -0.125 to 0.125
- key_projection_matrix: bfloat16 [2048, 512], P('wa'), may hold values from -0.125 to 0.125
- value_projection_matrix: bfloat16 [2048, 512], P('wa'), may hold values from -0.125 to 0.125
- output_weight: bfloat16 [4096, 2048], P('wa'), may hold values from -0.1875 to 0.1875
- attention_gain: bfloat16 [2048], P('wa'), may hold values from 0.5 to 1.5
- feedforward_gain: bfloat16 [2048], P('wa'), may hold values from 0.5 to 1.5
- query_gain: bfloat16 [128], P('wa'), may hold values from 0.796875 to 1.296875
- key_gain: bfloat16 [128], P('wa'), may hold values from 0.796875 to 1.296875
- expert_gate: bfloat16 [32, 2048, 768], P(('ctx', 'wa')), may hold values from -0.125 to 0.125
- expert_up: bfloat16 [32, 2048, 768], P(('ctx', 'wa')), may hold values from -0.125 to 0.125
- expert_down: bfloat16 [32, 768, 2048], P(('ctx', 'wa')), may hold values from -0.3125 to 0.3125
- expert_ids: int32 [8, 512, 8], P('wa', 'ctx'), may hold values from 0 to 31, all different within a row; in each aligned block of 128 rows (0 to 127, 128 to 255, ..., all dimensions but the last counted through in order) at most 64 rows name the same one
- route_gates: bfloat16 [8, 512, 8], P('wa', 'ctx'), may hold values from 0.25 to 1
- cotangent: float32 [8, 512, 2048], P('wa', 'ctx'), may hold values from -6 to 6
Outputs:
- block_output: float32 [8, 512, 2048], P('wa', 'ctx')
- input_grad: float32 [8, 512, 2048], P('wa', 'ctx')
- query_weight_grad: float32 [2048, 4096], P('wa')
- key_weight_grad: float32 [2048, 512], P('wa')
- value_weight_grad: float32 [2048, 512], P('wa')
- output_weight_grad: float32 [4096, 2048], P('wa')
- attention_gain_grad: float32 [2048], P('wa')
- feedforward_gain_grad: float32 [2048], P('wa')
- query_gain_grad: float32 [128], P('wa')
- key_gain_grad: float32 [128], P('wa')
- expert_gate_grad: float32 [32, 2048, 768], P(('ctx', 'wa'))
- expert_up_grad: float32 [32, 2048, 768], P(('ctx', 'wa'))
- expert_down_grad: float32 [32, 768, 2048], P(('ctx', 'wa'))
Inputs may be any that keep to these rules, and one draw needn't show every extreme that they name: `expert_ids`: each row names 8 different experts; the rows of one sequence block (128 rows in sequence order) name any one expert at most 64 times, a bound that some block reaches.
All inputs are finite; a program needn't handle non-finite values.
Results may differ from a plain program's by a relative error of at most 0.033.
Values may be sent and summed in bfloat16 or wider, within the bound.
No kernel may reach another device: no remote copies, remote signals or barrier semaphores. Data moves between devices by JAX's collectives and lax.ppermute only.
A program may use at most 320 MiB of HBM per device.

v0:
```python
import jax
import jax.numpy as jnp
from jax import lax
from jax.sharding import PartitionSpec as P

MODEL_WIDTH = 2048
QUERY_HEADS = 32
KEY_VALUE_HEADS = 4
HEAD_SIZE = 128
TOP = 8
EPSILON = 1e-06
ROPE_BASE = 1000000.0
VERY_NEGATIVE = -1e30
EVERY = ("ctx", "wa")


def inv_root(values):
    return lax.rsqrt(jnp.mean(values * values, axis=-1, keepdims=True) + EPSILON)


def rope_tables(positions):
    half_width = HEAD_SIZE // 2
    frequency = ROPE_BASE ** (-(jnp.arange(half_width).astype(positions.dtype) * 2.0 / HEAD_SIZE))
    angles = positions[:, None] * frequency[None, :]
    cosine, sine = (jnp.cos(angles), jnp.sin(angles))
    return (jnp.concatenate([cosine, cosine], axis=-1), jnp.concatenate([-sine, sine], axis=-1))


def swap_halves(values):
    half_width = values.shape[-1] // 2
    return jnp.concatenate([values[..., half_width:], values[..., :half_width]], axis=-1)


def rotate(values, cosine, sine):
    return values * cosine + swap_halves(values) * sine


def unrotate(values, cosine, sine):
    return values * cosine - swap_halves(values) * sine


def dot(a, b, contract):
    return lax.dot_general(a, b, (contract, ((), ())), preferred_element_type=jnp.float32)


def on_device(
    block_input,
    query_weight,
    key_projection_matrix,
    value_projection_matrix,
    output_weight,
    attention_gain,
    feedforward_gain,
    query_gain,
    key_gain,
    expert_gate,
    expert_up,
    expert_down,
    expert_ids,
    route_gates,
    cotangent,
):
    bf16, f32 = (jnp.bfloat16, jnp.float32)
    n_ctx, n_wa = (lax.axis_size("ctx"), lax.axis_size("wa"))
    my_ctx, my_wa = (lax.axis_index("ctx"), lax.axis_index("wa"))
    experts = n_ctx * n_wa
    block_rows = block_input[0]
    rows = block_rows.shape[0]
    length = rows * n_ctx
    capacity = 2 * rows * TOP // experts
    heads = QUERY_HEADS // n_ctx
    per_group = QUERY_HEADS // KEY_VALUE_HEADS
    sharers = per_group // heads
    head_columns = heads * HEAD_SIZE
    out_columns = MODEL_WIDTH // n_ctx
    score_scale = HEAD_SIZE ** (-0.5)
    gains = [attention_gain, feedforward_gain, query_gain, key_gain]
    small = jnp.concatenate(
        [expert_ids[0].astype(bf16).reshape(-1), route_gates[0].reshape(-1)] + gains
    )
    small = lax.all_gather(small, EVERY, axis=0)
    ids_all = small[:, : rows * TOP].reshape(experts, rows, TOP)
    gates_all = small[:, rows * TOP : 2 * rows * TOP].reshape(experts, rows, TOP)
    at = 2 * rows * TOP
    full_gains = []
    for g in gains:
        width = g.shape[0]
        full_gains.append(small[:n_wa, at : at + width].reshape(-1).astype(f32))
        at += width
    gain_attention, gain_feedforward, gain_query, gain_key = full_gains
    group = my_ctx * heads // per_group
    my_query = lax.dynamic_slice_in_dim(query_weight, my_ctx * head_columns, head_columns, 1)
    my_key = lax.dynamic_slice_in_dim(key_projection_matrix, group * HEAD_SIZE, HEAD_SIZE, 1)
    my_value = lax.dynamic_slice_in_dim(value_projection_matrix, group * HEAD_SIZE, HEAD_SIZE, 1)
    my_out = lax.dynamic_slice_in_dim(output_weight, my_ctx * out_columns, out_columns, 1)
    full_qkv = lax.all_gather(
        jnp.concatenate([my_query, my_key, my_value], axis=1), "wa", axis=0, tiled=True
    )
    full_out = lax.all_gather(my_out, "wa", axis=0, tiled=True)
    out_cotangent = cotangent[0]
    cot_all = lax.all_gather(out_cotangent.astype(bf16), EVERY, axis=0)
    root_x = inv_root(block_rows)
    x_hat = block_rows * root_x
    normed = (x_hat * gain_attention).astype(bf16)
    normed_all = lax.all_gather(normed, "ctx", axis=0, tiled=True)
    cosine, sine = rope_tables(jnp.arange(length, dtype=jnp.int32).astype(f32))
    qkv = dot(normed_all, full_qkv, ((1,), (0,)))
    query = qkv[:, :head_columns].reshape(length, heads, HEAD_SIZE).transpose(1, 0, 2)
    key_raw = qkv[:, head_columns : head_columns + HEAD_SIZE]
    value = qkv[:, head_columns + HEAD_SIZE :].astype(bf16)
    root_q = inv_root(query)
    q_hat = query * root_q
    root_k = inv_root(key_raw)
    k_hat = key_raw * root_k
    q_rot = rotate(q_hat * gain_query, cosine, sine).astype(bf16)
    k_rot = rotate(k_hat * gain_key, cosine, sine).astype(bf16)
    positions = jnp.arange(length, dtype=jnp.int32)
    allowed = positions[:, None] >= positions[None, :]
    scores = jnp.einsum("hqd,kd->hqk", q_rot, k_rot, preferred_element_type=f32) * score_scale
    masked = jnp.where(allowed, scores, VERY_NEGATIVE)
    top = jnp.max(masked, axis=-1, keepdims=True)
    weights = jnp.exp(masked - top)
    total = jnp.sum(weights, axis=-1, keepdims=True)
    attended = (
        jnp.einsum("hqk,kd->hqd", weights.astype(bf16), value, preferred_element_type=f32) / total
    ).astype(bf16)
    lse = top + jnp.log(total)
    attended_rows = attended.transpose(1, 0, 2).reshape(length, head_columns)
    attended_all = lax.all_gather(attended_rows, "ctx", axis=0)
    out_part = jnp.einsum(
        "ctk,ckn->tn",
        attended_all,
        full_out.reshape(n_ctx, head_columns, out_columns),
        preferred_element_type=f32,
    ).astype(bf16)
    out_rows = lax.all_to_all(
        out_part.reshape(n_ctx, rows, out_columns), "ctx", split_axis=0, concat_axis=0, tiled=True
    )
    hidden = block_rows + out_rows.transpose(1, 0, 2).reshape(rows, MODEL_WIDTH).astype(f32)
    root_h = inv_root(hidden)
    h_hat = hidden * root_h
    ffn_in = (h_hat * gain_feedforward).astype(bf16)
    ffn_all = lax.all_gather(ffn_in, EVERY, axis=0)
    me = (my_ctx * n_wa + my_wa).astype(bf16)
    mine = ids_all == me
    hit = jnp.any(mine, axis=-1)
    gate_of = jnp.sum(jnp.where(mine, gates_all.astype(f32), 0.0), axis=-1)
    token = jnp.arange(rows, dtype=jnp.int32)
    before = (token[:, None] < token[None, :]).astype(bf16)
    rank = dot(hit.astype(bf16), before, ((1,), (0,))).astype(jnp.int32)
    slot = jnp.arange(capacity, dtype=jnp.int32)
    chosen = (rank[:, None, :] == slot[None, :, None]) & hit[:, None, :]
    pick = chosen.astype(bf16)
    pick_gate = jnp.where(chosen, gate_of[:, None, :], 0.0).astype(bf16)
    gate_w, up_w, down_w = (expert_gate[0], expert_up[0], expert_down[0])

    def to_slots(one_hot, values):
        return (
            jnp.einsum("bst,btd->bsd", one_hot, values, preferred_element_type=f32)
            .astype(bf16)
            .reshape(experts * capacity, MODEL_WIDTH)
        )

    def to_tokens(one_hot, values):
        return (
            jnp.einsum(
                "bst,bsd->btd",
                one_hot,
                values.reshape(experts, capacity, MODEL_WIDTH),
                preferred_element_type=f32,
            )
            .astype(bf16)
            .reshape(experts * rows, MODEL_WIDTH)
        )

    down_grad = to_slots(pick_gate, cot_all)
    arrived = to_slots(pick, ffn_all)
    gate_pre = dot(arrived, gate_w, ((1,), (0,)))
    up_pre = dot(arrived, up_w, ((1,), (0,)))
    sigmoid_gate = jax.nn.sigmoid(gate_pre)
    activated = gate_pre * sigmoid_gate
    middle = (activated * up_pre).astype(bf16)
    d_middle = dot(down_grad, down_w, ((1,), (1,)))
    d_gate_pre = (
        d_middle * up_pre * sigmoid_gate * (1.0 + gate_pre * (1.0 - sigmoid_gate))
    ).astype(bf16)
    d_up_pre = (d_middle * activated).astype(bf16)
    d_rows = (dot(d_gate_pre, gate_w, ((1,), (1,))) + dot(d_up_pre, up_w, ((1,), (1,)))).astype(
        bf16
    )
    d_ffn = lax.psum_scatter(
        to_tokens(pick, d_rows), EVERY, scatter_dimension=0, tiled=True
    ).astype(f32)
    produced = dot(middle, down_w, ((1,), (0,))).astype(bf16)
    mixture = lax.psum_scatter(
        to_tokens(pick_gate, produced), EVERY, scatter_dimension=0, tiled=True
    ).astype(f32)
    block_output = hidden + mixture
    grad_down = dot(middle, down_grad, ((0,), (0,)))
    grad_gate = dot(arrived, d_gate_pre, ((0,), (0,)))
    grad_up = dot(arrived, d_up_pre, ((0,), (0,)))
    grad_feedforward = jnp.sum(d_ffn * h_hat, axis=0)
    grad_hat = d_ffn * gain_feedforward
    d_hidden = out_cotangent + root_h * (
        grad_hat - h_hat * jnp.mean(grad_hat * h_hat, axis=-1, keepdims=True)
    )
    d_out = lax.all_gather(d_hidden.astype(bf16), "ctx", axis=0, tiled=True)
    out_by_rows = lax.all_to_all(
        full_out.reshape(n_ctx, head_columns, out_columns),
        "ctx",
        split_axis=0,
        concat_axis=0,
        tiled=True,
    )
    d_attended = jnp.einsum(
        "tcn,ckn->tk",
        d_out.reshape(length, n_ctx, out_columns),
        out_by_rows,
        preferred_element_type=f32,
    ).astype(bf16)
    d_attended = d_attended.reshape(length, heads, HEAD_SIZE).transpose(1, 0, 2)
    delta = jnp.sum(d_attended.astype(f32) * attended.astype(f32), axis=-1, keepdims=True)
    scores = jnp.einsum("hqd,kd->hqk", q_rot, k_rot, preferred_element_type=f32) * score_scale
    probs = jnp.where(allowed, jnp.exp(scores - lse), 0.0)
    d_prob = jnp.einsum("hqd,kd->hqk", d_attended, value, preferred_element_type=f32)
    d_round = (probs * (d_prob - delta)).astype(bf16)
    d_value = jnp.einsum("hqk,hqd->kd", probs.astype(bf16), d_attended, preferred_element_type=f32)
    d_krot = jnp.einsum("hqk,hqd->kd", d_round, q_rot, preferred_element_type=f32) * score_scale
    d_qrot = jnp.einsum("hqk,kd->hqd", d_round, k_rot, preferred_element_type=f32) * score_scale
    d_qn = unrotate(d_qrot, cosine, sine)
    d_kn = unrotate(d_krot, cosine, sine)
    grad_qgain = jnp.sum(d_qn * q_hat, axis=(0, 1))
    grad_kgain = jnp.sum(d_kn * k_hat, axis=0)
    grad_q = d_qn * gain_query
    d_query = root_q * (grad_q - q_hat * jnp.mean(grad_q * q_hat, axis=-1, keepdims=True))
    grad_k = d_kn * gain_key
    d_key = root_k * (grad_k - k_hat * jnp.mean(grad_k * k_hat, axis=-1, keepdims=True))
    d_query = d_query.astype(bf16).transpose(1, 0, 2).reshape(length, head_columns)
    d_qkv = jnp.concatenate([d_query, d_key.astype(bf16), d_value.astype(bf16)], axis=1)
    d_normed = lax.psum_scatter(
        dot(d_qkv, full_qkv, ((1,), (1,))).astype(bf16), "ctx", scatter_dimension=0, tiled=True
    ).astype(f32)
    grad_attention = jnp.sum(d_normed * x_hat, axis=0)
    grad_n = d_normed * gain_attention
    input_grad = d_hidden + root_x * (
        grad_n - x_hat * jnp.mean(grad_n * x_hat, axis=-1, keepdims=True)
    )
    my_d_out = lax.dynamic_slice_in_dim(d_out, my_ctx * out_columns, out_columns, 1)
    grad_out = jnp.einsum("ctk,tn->ckn", attended_all, my_d_out, preferred_element_type=f32)
    grad_out = lax.psum_scatter(
        grad_out.astype(bf16).reshape(-1, out_columns), "wa", scatter_dimension=0, tiled=True
    )
    grad_out = lax.all_gather(grad_out, "ctx", axis=0)
    grad_out = grad_out.transpose(1, 0, 2).reshape(-1, MODEL_WIDTH).astype(f32)
    grad_qkv = dot(normed_all, d_qkv, ((0,), (0,))).astype(bf16)
    grad_qkv = lax.psum_scatter(grad_qkv, "wa", scatter_dimension=0, tiled=True)
    grad_qkv = lax.all_gather(grad_qkv, "ctx", axis=0).astype(f32)
    share = grad_qkv.shape[1]
    grad_query = (
        grad_qkv[:, :, :head_columns].transpose(1, 0, 2).reshape(share, QUERY_HEADS * HEAD_SIZE)
    )
    by_group = grad_qkv[:, :, head_columns:].reshape(KEY_VALUE_HEADS, sharers, share, 2, HEAD_SIZE)
    by_group = jnp.sum(by_group, axis=1)
    grad_key = by_group[:, :, 0].transpose(1, 0, 2).reshape(share, KEY_VALUE_HEADS * HEAD_SIZE)
    grad_value = by_group[:, :, 1].transpose(1, 0, 2).reshape(share, KEY_VALUE_HEADS * HEAD_SIZE)
    sums = lax.psum(
        jnp.concatenate([grad_attention, grad_feedforward, grad_qgain, grad_kgain]), EVERY
    )
    gain_grads, at = ([], 0)
    for g in gains:
        width = g.shape[0]
        gain_grads.append(lax.dynamic_slice_in_dim(sums, at + my_wa * width, width, 0))
        at += width * n_wa
    return (
        block_output[None],
        input_grad[None],
        grad_query,
        grad_key,
        grad_value,
        grad_out,
        *gain_grads,
        grad_gate[None],
        grad_up[None],
        grad_down[None],
    )


def solution(mesh):
    by_row, by_expert = (P("wa", None), P(EVERY, None, None))
    tokens = P("wa", "ctx", None)
    gain = P("wa")
    in_specs = (tokens,) + (by_row,) * 4 + (gain,) * 4 + (by_expert,) * 3 + (tokens,) * 3
    out_specs = (tokens,) * 2 + (by_row,) * 4 + (gain,) * 4 + (by_expert,) * 3
    return jax.shard_map(
        on_device, mesh=mesh, in_specs=in_specs, out_specs=out_specs, check_vma=False
    )
```

profile of v0, /device:TPU:0, one launch (start us, length us, event | category | flops | bytes accessed | tf_op | source)
XLA Modules:
  0.0 1365.4 jit_solution(2763674591959409322)
XLA Ops:
  14.5 124.3 %all-reduce.3.cloned.1.call-done = bf16[82944]{0:T(1024)(128)(2,1)} async-done(((bf16[82944]{0:T(1024)(128)(2,1)}), bf16[82944]{0:T(1024)(128)(2,1)}) %all-reduce.3.cloned.1.call-update) | async-done | bytes 165904
  151.3 29.5 %all-gather.13.cloned.1.call-done = bf16[512,2048]{1,0:T(8,128)(2,1)} async-done(((bf16[128,2048]{1,0:T(8,128)(2,1)}), bf16[512,2048]{1,0:T(8,128)(2,1)}) %all-gather.13.cloned.1.call-update) | async-done | bytes 2097168 | tf_op jit(solution)/shard_map/all_gather | solution.py:105
  180.8 58.3 %all-gather.15.cloned.1.call-done = bf16[2048,1280]{1,0:T(8,128)(2,1)} async-done(((bf16[256,1280]{1,0:T(8,128)(2,1)}), bf16[2048,1280]{1,0:T(8,128)(2,1)}) %all-gather.15.cloned.1.call-update) | async-done | bytes 5242896 | tf_op jit(solution)/shard_map/all_gather | solution.py:96
  274.1 13.1 all-gather.19.cloned.1.call-done
  287.1 53.7 %all-gather.17.cloned.1.call-done = bf16[4,512,1024]{2,1,0:T(8,128)(2,1)} async-done(((bf16[1,512,1024]{2,1,0:T(8,128)(2,1)}), bf16[4,512,1024]{2,1,0:T(8,128)(2,1)}) %all-gather.17.cloned.1.call-update) | async-done | bytes 4194320 | tf_op jit(solution)/shard_map/all_gather | solution.py:129
  351.6 12.0 all-to-all-done
  386.4 75.8 %all-gather.23.cloned.1.call-done = bf16[32,128,2048]{2,1,0:T(8,128)(2,1)} async-done(((bf16[1,128,2048]{2,1,0:T(8,128)(2,1)}), bf16[32,128,2048]{2,1,0:T(8,128)(2,1)}) %all-gather.23.cloned.1.call-update) | async-done | bytes 16777232 | tf_op jit(solution)/shard_map/all_gather | solution.py:101
  473.7 105.3 %all-gather.21.cloned.1.call-done = bf16[32,128,2048]{2,1,0:T(8,128)(2,1)} async-done(((bf16[1,128,2048]{2,1,0:T(8,128)(2,1)}), bf16[32,128,2048]{2,1,0:T(8,128)(2,1)}) %all-gather.21.cloned.1.call-update) | async-done | bytes 16777232 | tf_op jit(solution)/shard_map/all_gather | solution.py:143
  590.5 12.0 fusion.14
  611.1 13.9 %multiply_convert_fusion.1 = (bf16[2048,768]{1,0:T(8,128)(2,1)}, bf16[2048,768]{1,0:T(8,128)(2,1)}, bf16[2048,768]{1,0:T(8,128)(2,1)}) fusion(f32[2048,768]{1,0:T(8,128)} %fusion.18, f32[2048,768]{1,0:T(8,128)} %fusion.14, bf16[2048,2048]{1,0:T(8,128)(2,1)S(1)} %bitcast.194, bf16[1,768,2048]{2,1,0:T(8,128)(2,1)S(1)} %copy-done), kind=kOutput, calls=%fused_computation.12 | convolution fusion | flops 6466043904 | bytes 33554432 | tf_op jit(solution)/shard_map/dot_general | solution.py:43
  625.0 12.7 fusion.16
  637.7 12.9 add_convert_fusion
  650.5 13.7 %convolution_convert_fusion = bf16[32,128,2048]{2,1,0:T(8,128)(2,1)} fusion(bf16[32,64,2048]{2,1,0:T(8,128)(2,1)} %bitcast.190, s32[32,128]{1,0:T(8,128)S(1)} %convolution_convert_fusion.8, pred[32,128]{1,0:T(8,128)(4,1)S(1)} %copy.123), kind=kOutput, calls=%fused_computation.1 | convolution fusion | flops 1082654720 | bytes 25186304 | tf_op jit(solution)/shard_map/bst,bsd->btd/dot_general | solution.py:166
  664.3 184.9 %reduce-scatter.8.cloned.1.call-done = bf16[128,2048]{1,0:T(8,128)(2,1)} async-done(((bf16[4096,2048]{1,0:T(8,128)(2,1)}), bf16[128,2048]{1,0:T(8,128)(2,1)}) %reduce-scatter.8.cloned.1.call-update) | async-done | bytes 524304 | tf_op jit(solution)/shard_map/reduce_scatter | solution.py:191
  859.4 60.8 %all-gather.25.cloned.1.call-done = bf16[512,2048]{1,0:T(8,128)(2,1)} async-done(((bf16[128,2048]{1,0:T(8,128)(2,1)}), bf16[512,2048]{1,0:T(8,128)(2,1)}) %all-gather.25.cloned.1.call-update) | async-done | bytes 2097168 | tf_op jit(solution)/shard_map/all_gather | solution.py:207
  991.0 13.8 %convolution_convert_fusion.1 = bf16[32,128,2048]{2,1,0:T(8,128)(2,1)} fusion(bf16[32,64,2048]{2,1,0:T(8,128)(2,1)} %bitcast.189, bf16[32,128]{1,0:T(8,128)(2,1)S(1)} %copy-done.33, s32[32,128]{1,0:T(8,128)S(1)} %convolution_convert_fusion.8, pred[32,128]{1,0:T(8,128)(4,1)S(1)} %copy-done.29), kind=kOutput, calls=%fused_computation.2 | convolution fusion | flops 1082916864 | bytes 25194496 | tf_op jit(solution)/shard_map/bst,bsd->btd/dot_general | solution.py:166
  1005.5 12.4 convolution_bitcast_fusion.1
  1017.9 20.0 %reduce-scatter.12.cloned.1.call-done = bf16[256,1280]{1,0:T(8,128)(2,1)} async-done(((bf16[2048,1280]{1,0:T(8,128)(2,1)}), bf16[256,1280]{1,0:T(8,128)(2,1)}) %reduce-scatter.12.cloned.1.call-update) | async-done | bytes 655376 | tf_op jit(solution)/shard_map/reduce_scatter | solution.py:256
  1037.9 11.9 convolution_bitcast_fusion
  1061.0 13.8 %reduce-scatter.10.cloned.1.call-done = bf16[128,2048]{1,0:T(8,128)(2,1)} async-done(((bf16[512,2048]{1,0:T(8,128)(2,1)}), bf16[128,2048]{1,0:T(8,128)(2,1)}) %reduce-scatter.10.cloned.1.call-update) | async-done | bytes 524304 | tf_op jit(solution)/shard_map/reduce_scatter | solution.py:240
  1076.7 41.8 %psum.7 = f32[4352]{0:T(1024)S(1)} all-reduce(f32[4352]{0:T(1024)S(1)} %pad_maximum_fusion.6), channel_id=1, replica_groups=mesh['ctx'=4,'wa'=8] {'ctx','wa'}, use_global_device_ids=true, to_apply=%region_22.23 | all-reduce | flops 4352 | bytes 34816 | tf_op jit(solution)/shard_map/psum | solution.py:266
  1119.7 145.2 %reduce-scatter.6.cloned.1.call-done = bf16[128,2048]{1,0:T(8,128)(2,1)} async-done(((bf16[4096,2048]{1,0:T(8,128)(2,1)}), bf16[128,2048]{1,0:T(8,128)(2,1)}) %reduce-scatter.6.cloned.1.call-update) | async-done | bytes 524304 | tf_op jit(solution)/shard_map/reduce_scatter | solution.py:195
  1269.0 30.8 %all-gather.29.cloned.1.call-done = bf16[2048,512]{1,0:T(8,128)(2,1)} async-done(((bf16[512,512]{1,0:T(8,128)(2,1)}), bf16[2048,512]{1,0:T(8,128)(2,1)}) %all-gather.29.cloned.1.call-update) | async-done | bytes 2097168 | tf_op jit(solution)/shard_map/all_gather | solution.py:253
  1307.0 34.3 %all-gather.27.cloned.1.call-done = bf16[1024,1280]{1,0:T(8,128)(2,1)} async-done(((bf16[256,1280]{1,0:T(8,128)(2,1)}), bf16[1024,1280]{1,0:T(8,128)(2,1)}) %all-gather.27.cloned.1.call-update) | async-done | bytes 2621456 | tf_op jit(solution)/shard_map/all_gather | solution.py:257
  (293 shorter events, 243.5 us)
Async XLA Ops:
  7.2 603.9 %copy-start = (bf16[1,768,2048]{2,1,0:T(8,128)(2,1)S(1)}, bf16[1,768,2048]{2,1,0:T(8,128)(2,1)}, u32[]{:S(2)}) copy-start(bf16[1,768,2048]{2,1,0:T(8,128)(2,1)} %param.26) | copy-start | bytes 9437188
  7.2 131.5 %all-reduce.3.cloned.1.call-start = ((), (), s32[]{:S(2)}) async-start(), calls=%async_computation.21 | async-start | bytes 331776
  13.0 167.8 %all-gather.13.cloned.1.call-start = ((), (), s32[]{:S(2)}) async-start(), calls=%async_computation.7 | async-start | bytes 2621440 | tf_op jit(solution)/shard_map/all_gather | solution.py:105
  143.3 95.8 %all-gather.15.cloned.1.call-start = ((), (), s32[]{:S(2)}) async-start(), calls=%async_computation.8 | async-start | bytes 5898240 | tf_op jit(solution)/shard_map/all_gather | solution.py:96
  146.3 140.8 %all-gather.19.cloned.1.call-start = ((), (), s32[]{:S(2)}) async-start(), calls=%async_computation.10 | async-start | bytes 4718592 | tf_op jit(solution)/shard_map/all_gather | solution.py:99
  148.3 192.5 %all-gather.17.cloned.1.call-start = ((), (), s32[]{:S(2)}) async-start(), calls=%async_computation.9 | async-start | bytes 5242880 | tf_op jit(solution)/shard_map/all_gather | solution.py:129
  271.7 190.5 %all-gather.23.cloned.1.call-start = ((), (), s32[]{:S(2)}) async-start(), calls=%async_computation.13 | async-start | bytes 17301504 | tf_op jit(solution)/shard_map/all_gather | solution.py:101
  347.4 16.2 %all-to-all-start = ((bf16[4,128,512]{2,1,0:T(8,128)(2,1)}), bf16[4,128,512]{2,1,0:T(8,128)(2,1)}, u32[]{:S(2)}, u32[]{:S(2)}) async-start(bf16[4,128,512]{2,1,0:T(8,128)(2,1)} %bitcast.219), calls=%async_computation | async-start | bytes 1048576 | tf_op jit(solution)/shard_map/all_to_all | solution.py:136
  351.5 227.4 %all-gather.21.cloned.1.call-start = ((), (), s32[]{:S(2)}) async-start(), calls=%async_computation.11 | async-start | bytes 17301504 | tf_op jit(solution)/shard_map/all_gather | solution.py:143
  351.6 500.0 %copy-start.34 = (f32[1,2,8,128]{3,1,2,0:T(2,128)}, f32[1,2,8,128]{3,1,2,0:T(2,128)S(1)}, u32[]{:S(2)}) copy-start(f32[1,2,8,128]{3,1,2,0:T(2,128)S(1)} %copy.165) | copy-start | bytes 24580
  374.3 477.4 %copy-start.53 = (f32[128]{0:T(128)}, f32[128]{0:T(128)S(1)}, u32[]{:S(2)}) copy-start(f32[128]{0:T(128)S(1)} %add_rsqrt_fusion.2) | copy-start | bytes 1540
  375.3 474.0 %reduce-scatter.8.cloned.1.call-start = ((), (), s32[]{:S(2)}) async-start(), calls=%async_computation.14 | async-start | bytes 17301504 | tf_op jit(solution)/shard_map/reduce_scatter | solution.py:191
  379.4 271.1 %copy-start.28 = (pred[32,128]{1,0:T(8,128)(4,1)}, pred[32,128]{1,0:T(8,128)(4,1)S(1)}, u32[]{:S(2)}) copy-start(pred[32,128]{1,0:T(8,128)(4,1)S(1)} %copy.123) | copy-start | bytes 12292
  664.3 255.9 %all-gather.25.cloned.1.call-start = ((), (), s32[]{:S(2)}) async-start(), calls=%async_computation.15 | async-start | bytes 2621440 | tf_op jit(solution)/shard_map/all_gather | solution.py:207
  854.5 78.4 %all-to-all-start.1 = ((bf16[4,1024,512]{2,1,0:T(8,128)(2,1)}), bf16[4,1024,512]{2,1,0:T(8,128)(2,1)}, u32[]{:S(2)}, u32[]{:S(2)}) async-start(bf16[4,1024,512]{2,1,0:T(8,128)(2,1)} %bitcast.205), calls=%async_computation.3 | async-start | bytes 8388608 | tf_op jit(solution)/shard_map/all_to_all | solution.py:208
  859.4 145.6 %reduce-scatter.14.cloned.1.call-start = ((), (), s32[]{:S(2)}) async-start(), calls=%async_computation.18 | async-start | bytes 4718592 | tf_op jit(solution)/shard_map/reduce_scatter | solution.py:250
  926.9 110.9 %reduce-scatter.12.cloned.1.call-start = ((), (), s32[]{:S(2)}) async-start(), calls=%async_computation.17 | async-start | bytes 5898240 | tf_op jit(solution)/shard_map/reduce_scatter | solution.py:256
  972.0 102.8 %reduce-scatter.10.cloned.1.call-start = ((), (), s32[]{:S(2)}) async-start(), calls=%async_computation.16 | async-start | bytes 2621440 | tf_op jit(solution)/shard_map/reduce_scatter | solution.py:240
  980.1 284.9 %reduce-scatter.6.cloned.1.call-start = ((), (), s32[]{:S(2)}) async-start(), calls=%async_computation.12 | async-start | bytes 17301504 | tf_op jit(solution)/shard_map/reduce_scatter | solution.py:195
  1004.9 295.0 %all-gather.29.cloned.1.call-start = ((), (), s32[]{:S(2)}) async-start(), calls=%async_computation.20 | async-start | bytes 2621440 | tf_op jit(solution)/shard_map/all_gather | solution.py:253
  1005.5 335.9 %all-gather.27.cloned.1.call-start = ((), (), s32[]{:S(2)}) async-start(), calls=%async_computation.19 | async-start | bytes 3276800 | tf_op jit(solution)/shard_map/all_gather | solution.py:257
  1049.8 215.1 %copy-start.35 = (f32[1,2,8,128]{3,1,2,0:T(2,128)S(1)}, f32[1,2,8,128]{3,1,2,0:T(2,128)}, u32[]{:S(2)}) copy-start(f32[1,2,8,128]{3,1,2,0:T(2,128)} %copy-done.34) | copy-start | bytes 24580
  1049.9 215.1 %copy-start.54 = (f32[128]{0:T(128)S(1)}, f32[128]{0:T(128)}, u32[]{:S(2)}) copy-start(f32[128]{0:T(128)} %copy-done.53) | copy-start | bytes 1540
  1049.9 215.1 %copy-start.58 = (f32[128]{0:T(128)S(1)}, f32[128]{0:T(128)}, u32[]{:S(2)}) copy-start(f32[128]{0:T(128)} %copy-done.57) | copy-start | bytes 1540
  (66 other events, 826.0 us)
Sparse Core Ops, SparseCore 0:
  14.1 124.5 all-reduce.2
  143.5 37.2 all-gather.12
  183.0 56.0 all-gather.14
  241.1 45.9 all-gather.18
  289.4 51.3 all-gather.16
  344.2 117.9 all-gather.22
  465.8 113.0 all-gather.20
  664.4 184.7 reduce-scatter.7
  854.6 65.5 all-gather.24
  927.0 49.7 reduce-scatter.13
  979.8 58.0 reduce-scatter.11
  1041.2 33.5 reduce-scatter.9
  1077.2 187.6 reduce-scatter.5
  1266.8 33.0 all-gather.28
  1301.7 39.6 all-gather.26
where the time goes:
time: 1380 us; the launch traced here: 1370 us
  waiting for transfers between devices  962 us (70%)
  matrix products  213 us (15%)
  local copies, waits for them, and re-layouts  70.5 us (5%)
  other arithmetic  52.6 us (4%)
  blocking collectives  41.8 us (3%)
  between operations  15 us (1%)
    reduce_scatter x1, waiting for transfers between devices, on_device(): lax.psum_scatter(to_tokens(pick, d_rows), EVERY, scatter_dimension=0, til...  185 us
    reduce_scatter x1, waiting for transfers between devices, on_device(): lax.psum_scatter(to_tokens(pick_gate, produced), EVERY, scatter_dimension...  145 us
    dot_general x13, matrix products, dot(): lax.dot_general(a, b, (contract, ((), ())), preferred_element_type=jnp.fl...  125 us
    unnamed x16, waiting for transfers between devices  125 us
    all_gather x1, waiting for transfers between devices, on_device(): ffn_all = lax.all_gather(ffn_in, EVERY, axis=0)  105 us
    all_gather x1, waiting for transfers between devices, on_device(): cot_all = lax.all_gather(out_cotangent.astype(bf16), EVERY, axis=0)  75.8 us
    all_gather x1, waiting for transfers between devices, on_device(): d_out = lax.all_gather(d_hidden.astype(bf16), 'ctx', axis=0, tiled=True)  60.8 us
    all_gather x1, waiting for transfers between devices, on_device(): lax.all_gather(jnp.concatenate([my_query, my_key, my_value], axis=1), 'wa...  58.3 us
  transfers between devices with their start and end apart: 17, of which 15 were waited for; matrix products, arithmetic and copies ran while one was open for 15% of the time, Pallas kernels for 0%

commit v1 on v0

--- a/solution.py
+++ b/solution.py
@@ -102,7 +102,13 @@
     root_x = inv_root(block_rows)
     x_hat = block_rows * root_x
     normed = (x_hat * gain_attention).astype(bf16)
-    normed_all = lax.all_gather(normed, "ctx", axis=0, tiled=True)
+    size = lax.axis_size("ctx")
+    current, tiles = (normed, [normed])
+    for _ in range(size - 1):
+        current = lax.ppermute(current, "ctx", [(i, (i + 1) % size) for i in range(size)])
+        tiles.insert(0, current)
+    line = jnp.concatenate(tiles, axis=0)
+    normed_all = jnp.roll(line, (lax.axis_index("ctx") + 1) * normed.shape[0], axis=0)
     cosine, sine = rope_tables(jnp.arange(length, dtype=jnp.int32).astype(f32))
     qkv = dot(normed_all, full_qkv, ((1,), (0,)))
     query = qkv[:, :head_columns].reshape(length, heads, HEAD_SIZE).transpose(1, 0, 2)

time: 1380 us -> 1360 us (0.986)
  waiting for transfers between devices: 962 us -> 920 us
    all_gather x1, waiting for transfers between devices: 58.3 us -> 0.01 us  [on_device(): lax.all_gather(jnp.concatenate([my_query, my_key, my_value], axis=1), 'wa...]
    ppermute x0 -> x3, waiting for transfers between devices: none -> 36.5 us  [on_device(): lax.ppermute(current, 'ctx', [(i, (i + 1) % size) for i in range(size)])]
    unnamed x16 -> x15, waiting for transfers between devices: 125 us -> 157 us
    all_gather x1 -> x0, waiting for transfers between devices: 29.5 us -> none  [on_device(): normed_all = lax.all_gather(normed, 'ctx', axis=0, tiled=True)]
  transfers between devices with their start and end apart: 17 -> 19, of which waited for: 15 -> 15; matrix products, arithmetic and copies ran while one was open for 15% -> 17% of each run, Pallas kernels for 0% -> 0%
where the time goes in v1:
time: 1360 us; the launch traced here: 1340 us
  waiting for transfers between devices  920 us (68%)
  matrix products  216 us (16%)
  local copies, waits for them, and re-layouts  79.4 us (6%)
  other arithmetic  56.6 us (4%)
  blocking collectives  42 us (3%)
  between operations  17.1 us (1%)
    reduce_scatter x1, waiting for transfers between devices, on_device(): lax.psum_scatter(to_tokens(pick, d_rows), EVERY, scatter_dimension=0, til...  185 us
    unnamed x15, waiting for transfers between devices  157 us
    reduce_scatter x1, waiting for transfers between devices, on_device(): lax.psum_scatter(to_tokens(pick_gate, produced), EVERY, scatter_dimension...  145 us
    dot_general x13, matrix products, dot(): lax.dot_general(a, b, (contract, ((), ())), preferred_element_type=jnp.fl...  127 us
    all_gather x1, waiting for transfers between devices, on_device(): ffn_all = lax.all_gather(ffn_in, EVERY, axis=0)  105 us
    all_gather x1, waiting for transfers between devices, on_device(): cot_all = lax.all_gather(out_cotangent.astype(bf16), EVERY, axis=0)  75.5 us
    all_gather x1, waiting for transfers between devices, on_device(): d_out = lax.all_gather(d_hidden.astype(bf16), 'ctx', axis=0, tiled=True)  60.7 us
    all_gather x1, waiting for transfers between devices, on_device(): attended_all = lax.all_gather(attended_rows, 'ctx', axis=0)  48 us
  transfers between devices with their start and end apart: 19, of which 15 were waited for; matrix products, arithmetic and copies ran while one was open for 17% of the time, Pallas kernels for 0%

profile of v1, /device:TPU:0, one launch (start us, length us, event | category | flops | bytes accessed | tf_op | source)
XLA Modules:
  0.0 1344.1 jit_solution(8932586800063248973)
XLA Ops:
  18.3 156.8 %all-reduce.3.cloned.1.call-done = bf16[82944]{0:T(1024)(128)(2,1)} async-done(((bf16[82944]{0:T(1024)(128)(2,1)}), bf16[82944]{0:T(1024)(128)(2,1)}) %all-reduce.3.cloned.1.call-update) | async-done | bytes 165904
  179.8 13.7 %collective-permute-done = bf16[128,2048]{1,0:T(8,128)(2,1)} collective-permute-done((bf16[128,2048]{1,0:T(8,128)(2,1)S(1)}, bf16[128,2048]{1,0:T(8,128)(2,1)}, u32[]{:S(2)}, u32[]{:S(2)}) %collective-permute-start) | collective-permute-done | bytes 524320 | tf_op jit(solution)/shard_map/ppermute | solution.py:108
  196.2 12.0 collective-permute-done.1
  271.7 48.0 %all-gather.14.cloned.1.call-done = bf16[4,512,1024]{2,1,0:T(8,128)(2,1)} async-done(((bf16[1,512,1024]{2,1,0:T(8,128)(2,1)}), bf16[4,512,1024]{2,1,0:T(8,128)(2,1)}) %all-gather.14.cloned.1.call-update) | async-done | bytes 4194320 | tf_op jit(solution)/shard_map/all_gather | solution.py:135
  330.5 11.9 all-to-all-done
  365.3 75.5 %all-gather.20.cloned.1.call-done = bf16[32,128,2048]{2,1,0:T(8,128)(2,1)} async-done(((bf16[1,128,2048]{2,1,0:T(8,128)(2,1)}), bf16[32,128,2048]{2,1,0:T(8,128)(2,1)}) %all-gather.20.cloned.1.call-update) | async-done | bytes 16777232 | tf_op jit(solution)/shard_map/all_gather | solution.py:101
  452.2 105.2 %all-gather.18.cloned.1.call-done = bf16[32,128,2048]{2,1,0:T(8,128)(2,1)} async-done(((bf16[1,128,2048]{2,1,0:T(8,128)(2,1)}), bf16[32,128,2048]{2,1,0:T(8,128)(2,1)}) %all-gather.18.cloned.1.call-update) | async-done | bytes 16777232 | tf_op jit(solution)/shard_map/all_gather | solution.py:149
  557.4 11.5 convolution_convert_fusion.5
  568.9 12.2 fusion.14
  589.6 13.9 %multiply_convert_fusion.1 = (bf16[2048,768]{1,0:T(8,128)(2,1)}, bf16[2048,768]{1,0:T(8,128)(2,1)}, bf16[2048,768]{1,0:T(8,128)(2,1)}) fusion(f32[2048,768]{1,0:T(8,128)} %fusion.18, f32[2048,768]{1,0:T(8,128)} %fusion.14, bf16[2048,2048]{1,0:T(8,128)(2,1)S(1)} %bitcast.196, bf16[1,768,2048]{2,1,0:T(8,128)(2,1)S(1)} %copy-done), kind=kOutput, calls=%fused_computation.12 | convolution fusion | flops 6466043904 | bytes 33554432 | tf_op jit(solution)/shard_map/dot_general | solution.py:43
  603.5 12.8 fusion.16
  616.4 12.6 add_convert_fusion
  628.9 13.7 %convolution_convert_fusion = bf16[32,128,2048]{2,1,0:T(8,128)(2,1)} fusion(bf16[32,64,2048]{2,1,0:T(8,128)(2,1)} %bitcast.192, s32[32,128]{1,0:T(8,128)S(1)} %convolution_convert_fusion.8, pred[32,128]{1,0:T(8,128)(4,1)S(1)} %copy.123), kind=kOutput, calls=%fused_computation.1 | convolution fusion | flops 1082654720 | bytes 25186304 | tf_op jit(solution)/shard_map/bst,bsd->btd/dot_general | solution.py:172
  642.7 184.9 %reduce-scatter.8.cloned.1.call-done = bf16[128,2048]{1,0:T(8,128)(2,1)} async-done(((bf16[4096,2048]{1,0:T(8,128)(2,1)}), bf16[128,2048]{1,0:T(8,128)(2,1)}) %reduce-scatter.8.cloned.1.call-update) | async-done | bytes 524304 | tf_op jit(solution)/shard_map/reduce_scatter | solution.py:197
  837.8 60.7 %all-gather.22.cloned.1.call-done = bf16[512,2048]{1,0:T(8,128)(2,1)} async-done(((bf16[128,2048]{1,0:T(8,128)(2,1)}), bf16[512,2048]{1,0:T(8,128)(2,1)}) %all-gather.22.cloned.1.call-update) | async-done | bytes 2097168 | tf_op jit(solution)/shard_map/all_gather | solution.py:213
  972.9 13.8 %convolution_convert_fusion.1 = bf16[32,128,2048]{2,1,0:T(8,128)(2,1)} fusion(bf16[32,64,2048]{2,1,0:T(8,128)(2,1)} %bitcast.191, bf16[32,128]{1,0:T(8,128)(2,1)S(1)} %copy-done.35, s32[32,128]{1,0:T(8,128)S(1)} %convolution_convert_fusion.8, pred[32,128]{1,0:T(8,128)(4,1)S(1)} %copy-done.29), kind=kOutput, calls=%fused_computation.2 | convolution fusion | flops 1082916864 | bytes 25194496 | tf_op jit(solution)/shard_map/bst,bsd->btd/dot_general | solution.py:172
  987.6 12.0 convolution_bitcast_fusion.1
  999.6 16.2 %reduce-scatter.12.cloned.1.call-done = bf16[256,1280]{1,0:T(8,128)(2,1)} async-done(((bf16[2048,1280]{1,0:T(8,128)(2,1)}), bf16[256,1280]{1,0:T(8,128)(2,1)}) %reduce-scatter.12.cloned.1.call-update) | async-done | bytes 655376 | tf_op jit(solution)/shard_map/reduce_scatter | solution.py:262
  1015.8 11.9 convolution_bitcast_fusion
  1039.0 13.7 %reduce-scatter.10.cloned.1.call-done = bf16[128,2048]{1,0:T(8,128)(2,1)} async-done(((bf16[512,2048]{1,0:T(8,128)(2,1)}), bf16[128,2048]{1,0:T(8,128)(2,1)}) %reduce-scatter.10.cloned.1.call-update) | async-done | bytes 524304 | tf_op jit(solution)/shard_map/reduce_scatter | solution.py:246
  1054.5 42.0 %psum.7 = f32[4352]{0:T(1024)S(1)} all-reduce(f32[4352]{0:T(1024)S(1)} %pad_maximum_fusion.6), channel_id=1, replica_groups=mesh['ctx'=4,'wa'=8] {'ctx','wa'}, use_global_device_ids=true, to_apply=%region_22.23 | all-reduce | flops 4352 | bytes 34816 | tf_op jit(solution)/shard_map/psum | solution.py:272
  1097.8 144.9 %reduce-scatter.6.cloned.1.call-done = bf16[128,2048]{1,0:T(8,128)(2,1)} async-done(((bf16[4096,2048]{1,0:T(8,128)(2,1)}), bf16[128,2048]{1,0:T(8,128)(2,1)}) %reduce-scatter.6.cloned.1.call-update) | async-done | bytes 524304 | tf_op jit(solution)/shard_map/reduce_scatter | solution.py:201
  1246.7 30.6 %all-gather.26.cloned.1.call-done = bf16[2048,512]{1,0:T(8,128)(2,1)} async-done(((bf16[512,512]{1,0:T(8,128)(2,1)}), bf16[2048,512]{1,0:T(8,128)(2,1)}) %all-gather.26.cloned.1.call-update) | async-done | bytes 2097168 | tf_op jit(solution)/shard_map/all_gather | solution.py:259
  1284.5 34.3 %all-gather.24.cloned.1.call-done = bf16[1024,1280]{1,0:T(8,128)(2,1)} async-done(((bf16[256,1280]{1,0:T(8,128)(2,1)}), bf16[1024,1280]{1,0:T(8,128)(2,1)}) %all-gather.24.cloned.1.call-update) | async-done | bytes 2621456 | tf_op jit(solution)/shard_map/all_gather | solution.py:263
  (302 shorter events, 262.0 us)
Async XLA Ops:
  8.0 581.6 %copy-start = (bf16[1,768,2048]{2,1,0:T(8,128)(2,1)S(1)}, bf16[1,768,2048]{2,1,0:T(8,128)(2,1)}, u32[]{:S(2)}) copy-start(bf16[1,768,2048]{2,1,0:T(8,128)(2,1)} %param.26) | copy-start | bytes 9437188
  8.0 167.0 %all-reduce.3.cloned.1.call-start = ((), (), s32[]{:S(2)}) async-start(), calls=%async_computation.20 | async-start | bytes 331776
  13.8 222.4 %all-gather.12.cloned.1.call-start = ((), (), s32[]{:S(2)}) async-start(), calls=%async_computation.7 | async-start | bytes 5898240 | tf_op jit(solution)/shard_map/all_gather | solution.py:96
  16.8 254.9 %all-gather.16.cloned.1.call-start = ((), (), s32[]{:S(2)}) async-start(), calls=%async_computation.9 | async-start | bytes 4718592 | tf_op jit(solution)/shard_map/all_gather | solution.py:99
  18.2 217.0 %copy-start.49 = (f32[128]{0:T(128)}, f32[128]{0:T(128)S(1)}, u32[]{:S(2)}) copy-start(f32[128]{0:T(128)S(1)} %add_rsqrt_fusion.3) | copy-start | bytes 1540
  178.3 15.3 %collective-permute-start = (bf16[128,2048]{1,0:T(8,128)(2,1)S(1)}, bf16[128,2048]{1,0:T(8,128)(2,1)}, u32[]{:S(2)}, u32[]{:S(2)}) collective-permute-start(bf16[128,2048]{1,0:T(8,128)(2,1)S(1)} %multiply_convert_fusion.6), channel_id=1, source_target_pairs={{0,8},{8,16},{16,24},{24,0},{1,9},{9,17},{17,25},{25,1},{2,10},{10... | collective-permute-start | bytes 1572872 | tf_op jit(solution)/shard_map/ppermute | solution.py:108
  193.5 14.6 %collective-permute-start.1 = (bf16[128,2048]{1,0:T(8,128)(2,1)}, bf16[128,2048]{1,0:T(8,128)(2,1)}, u32[]{:S(2)}, u32[]{:S(2)}) collective-permute-start(bf16[128,2048]{1,0:T(8,128)(2,1)} %collective-permute-done), channel_id=1, source_target_pairs={{0,8},{8,16},{16,24},{24,0},{1,9},{9,17},{17,25},{25,1},{2,10},{10... | collective-permute-start | bytes 1572872 | tf_op jit(solution)/shard_map/ppermute | solution.py:108
  196.0 123.7 %all-gather.14.cloned.1.call-start = ((), (), s32[]{:S(2)}) async-start(), calls=%async_computation.8 | async-start | bytes 5242880 | tf_op jit(solution)/shard_map/all_gather | solution.py:135
  208.1 13.7 %collective-permute-start.2 = (bf16[128,2048]{1,0:T(8,128)(2,1)}, bf16[128,2048]{1,0:T(8,128)(2,1)}, u32[]{:S(2)}, u32[]{:S(2)}) collective-permute-start(bf16[128,2048]{1,0:T(8,128)(2,1)} %collective-permute-done.1), channel_id=1, source_target_pairs={{0,8},{8,16},{16,24},{24,0},{1,9},{9,17},{17,25},{25,1},{2,10},{10... | collective-permute-start | bytes 1572872 | tf_op jit(solution)/shard_map/ppermute | solution.py:108
  269.3 171.5 %all-gather.20.cloned.1.call-start = ((), (), s32[]{:S(2)}) async-start(), calls=%async_computation.12 | async-start | bytes 17301504 | tf_op jit(solution)/shard_map/all_gather | solution.py:101
  326.3 16.2 %all-to-all-start = ((bf16[4,128,512]{2,1,0:T(8,128)(2,1)}), bf16[4,128,512]{2,1,0:T(8,128)(2,1)}, u32[]{:S(2)}, u32[]{:S(2)}) async-start(bf16[4,128,512]{2,1,0:T(8,128)(2,1)} %bitcast.221), calls=%async_computation | async-start | bytes 1048576 | tf_op jit(solution)/shard_map/all_to_all | solution.py:142
  330.4 226.9 %all-gather.18.cloned.1.call-start = ((), (), s32[]{:S(2)}) async-start(), calls=%async_computation.10 | async-start | bytes 17301504 | tf_op jit(solution)/shard_map/all_gather | solution.py:149
  330.5 499.5 %copy-start.36 = (f32[1,2,8,128]{3,1,2,0:T(2,128)}, f32[1,2,8,128]{3,1,2,0:T(2,128)S(1)}, u32[]{:S(2)}) copy-start(f32[1,2,8,128]{3,1,2,0:T(2,128)S(1)} %copy.165) | copy-start | bytes 24580
  353.1 477.0 %copy-start.55 = (f32[128]{0:T(128)}, f32[128]{0:T(128)S(1)}, u32[]{:S(2)}) copy-start(f32[128]{0:T(128)S(1)} %add_rsqrt_fusion.2) | copy-start | bytes 1540
  354.1 473.6 %reduce-scatter.8.cloned.1.call-start = ((), (), s32[]{:S(2)}) async-start(), calls=%async_computation.13 | async-start | bytes 17301504 | tf_op jit(solution)/shard_map/reduce_scatter | solution.py:197
  358.2 270.7 %copy-start.28 = (pred[32,128]{1,0:T(8,128)(4,1)}, pred[32,128]{1,0:T(8,128)(4,1)S(1)}, u32[]{:S(2)}) copy-start(pred[32,128]{1,0:T(8,128)(4,1)S(1)} %copy.123) | copy-start | bytes 12292
  642.7 255.9 %all-gather.22.cloned.1.call-start = ((), (), s32[]{:S(2)}) async-start(), calls=%async_computation.14 | async-start | bytes 2621440 | tf_op jit(solution)/shard_map/all_gather | solution.py:213
  832.9 78.2 %all-to-all-start.1 = ((bf16[4,1024,512]{2,1,0:T(8,128)(2,1)}), bf16[4,1024,512]{2,1,0:T(8,128)(2,1)}, u32[]{:S(2)}, u32[]{:S(2)}) async-start(bf16[4,1024,512]{2,1,0:T(8,128)(2,1)} %bitcast.207), calls=%async_computation.3 | async-start | bytes 8388608 | tf_op jit(solution)/shard_map/all_to_all | solution.py:214
  837.8 149.0 %reduce-scatter.14.cloned.1.call-start = ((), (), s32[]{:S(2)}) async-start(), calls=%async_computation.17 | async-start | bytes 4718592 | tf_op jit(solution)/shard_map/reduce_scatter | solution.py:256
  905.3 110.5 %reduce-scatter.12.cloned.1.call-start = ((), (), s32[]{:S(2)}) async-start(), calls=%async_computation.16 | async-start | bytes 5898240 | tf_op jit(solution)/shard_map/reduce_scatter | solution.py:262
  953.9 98.8 %reduce-scatter.10.cloned.1.call-start = ((), (), s32[]{:S(2)}) async-start(), calls=%async_computation.15 | async-start | bytes 2621440 | tf_op jit(solution)/shard_map/reduce_scatter | solution.py:246
  961.9 280.8 %reduce-scatter.6.cloned.1.call-start = ((), (), s32[]{:S(2)}) async-start(), calls=%async_computation.11 | async-start | bytes 17301504 | tf_op jit(solution)/shard_map/reduce_scatter | solution.py:201
  986.8 290.6 %all-gather.26.cloned.1.call-start = ((), (), s32[]{:S(2)}) async-start(), calls=%async_computation.19 | async-start | bytes 2621440 | tf_op jit(solution)/shard_map/all_gather | solution.py:259
  987.3 331.5 %all-gather.24.cloned.1.call-start = ((), (), s32[]{:S(2)}) async-start(), calls=%async_computation.18 | async-start | bytes 3276800 | tf_op jit(solution)/shard_map/all_gather | solution.py:263
  (67 other events, 1308.7 us)
Sparse Core Ops, SparseCore 0:
  15.0 159.9 all-reduce.2
  642.8 184.8 reduce-scatter.7
Sparse Core Ops, SparseCore 1:
  16.9 59.0 all-gather.11
  196.1 46.9 all-gather.15
  269.4 50.3 all-gather.13
  323.3 117.4 all-gather.19
  444.4 112.9 all-gather.17
  833.0 65.5 all-gather.21
  905.4 49.7 reduce-scatter.13
  957.8 57.9 reduce-scatter.11
  1019.2 33.5 reduce-scatter.9
  1055.1 187.4 reduce-scatter.5
  1244.5 32.8 all-gather.25
  1279.4 39.4 all-gather.23
